TPU v7x, 128 devices: a whole 4x4x4 slice. The times are simulated.
128 devices in a mesh: phase: 4 (over z_hi, core), dp: 32 (over x, y, z_lo).
Axes of the slice: x: 4, y: 4, z: 4 (z_hi: 2, z_lo: 2; z = z_hi * 2 + z_lo), core: 2. Of those that a mesh axis runs over, the one named last changes fastest.
Arguments:
- query_key_value_blocks: bfloat16 [4, 32, 2, 128, 10240], P('phase', 'dp'), may hold values from -18 to 18
- row_document_index: int32 [4, 32, 2, 128], P('phase', 'dp'), may hold values from 0 to 3, never falling along the last dimension, each value on 1 to 64 neighbouring positions
- counts: int32 [4, 32], P('phase', 'dp'), may hold values from 1 to 2
- block_adapter_index: int32 [4, 32, 2], P('phase'), may hold values from 0 to 31
- lowrank_down_weight: bfloat16 [4, 32, 8192, 64], P('phase', None, 'dp'), may hold values from -0.0625 to 0.0625
- lowrank_up_weight: bfloat16 [4, 32, 64, 8192], P('phase', None, None, 'dp'), may hold values from -0.75 to 0.75
- cotangent: bfloat16 [4, 32, 2, 128, 8192], P('phase', None, None, None, 'dp'), may hold values from -0.1796875 to 0.1796875
Outputs:
- delta: bfloat16 [4, 32, 2, 128, 8192], P('phase', None, None, None, 'dp')
- grad_down: float32 [4, 32, 8192, 64], P('phase', None, 'dp')
- grad_up: float32 [4, 32, 64, 8192], P('phase', None, None, 'dp')
Inputs may be any that keep to these rules, and one draw needn't show every extreme that they name: `row_document_index`: each row lies in one document; documents of a block are consecutive rows, at most 64 rows each.
All inputs are finite; a program needn't handle non-finite values.
Results may differ from a plain program's by a relative error of at most 0.0061.
Values may be sent and summed in bfloat16 or wider, within the bound.
A program may use at most 128 MiB of HBM per device.

v0:
```python
import jax
import jax.numpy as jnp
from jax import lax
from jax.sharding import PartitionSpec as P

HEADS = 64
KV_HEADS = 8
HEAD_DIM = 128


LOWRANK_SCALE = 2.0


def shifted(array, axis, by):
    peers = lax.axis_size(axis)
    return lax.ppermute(array, axis, [(i, (i + by) % peers) for i in range(peers)])


def attend(qkv_rows, documents, alive_mask):
    slot_count = qkv_rows.shape[0]
    block_rows = qkv_rows.shape[1]
    group_size = HEADS // KV_HEADS
    queries = qkv_rows[:, :, : HEADS * HEAD_DIM].reshape(
        slot_count, block_rows, KV_HEADS, group_size, HEAD_DIM
    )
    key_rows = qkv_rows[:, :, HEADS * HEAD_DIM : (HEADS + KV_HEADS) * HEAD_DIM].reshape(
        slot_count, block_rows, KV_HEADS, HEAD_DIM
    )
    value_rows = qkv_rows[:, :, (HEADS + KV_HEADS) * HEAD_DIM :].reshape(
        slot_count, block_rows, KV_HEADS, HEAD_DIM
    )
    scores = jnp.einsum(
        "sikgd,sjkd->skgij", queries, key_rows, preferred_element_type=jnp.float32
    ) * HEAD_DIM ** (-0.5)
    position = jnp.arange(block_rows)
    allowed = (documents[:, :, None] == documents[:, None, :]) & (
        position[None, None, :] <= position[None, :, None]
    )
    scores = jnp.where(allowed[:, None, None, :, :], scores, -1e30)
    row_max = jnp.max(scores, axis=-1, keepdims=True)
    powers = jnp.exp(scores - row_max)
    weights = (powers / jnp.sum(powers, axis=-1, keepdims=True)).astype(jnp.bfloat16)
    mixed = jnp.einsum("skgij,sjkd->sikgd", weights, value_rows, preferred_element_type=jnp.float32)
    mixed = mixed.reshape(slot_count, block_rows, HEADS * HEAD_DIM)
    return (mixed * alive_mask[:, None, None]).astype(jnp.bfloat16)


def on_device(
    query_key_value_blocks,
    row_document_index,
    counts,
    block_adapter_index,
    lowrank_down_weight,
    lowrank_up_weight,
    cotangent,
):
    slot_index = jnp.arange(query_key_value_blocks.shape[2])
    selected_up_weight = jnp.take(lowrank_up_weight[0], block_adapter_index[0], axis=0)
    grad_rows = cotangent[0]
    back_part = jnp.einsum(
        "psiw,psrw->psir", grad_rows, selected_up_weight, preferred_element_type=jnp.float32
    )
    backward_rows = lax.psum(back_part, "dp")
    arriving = shifted(query_key_value_blocks, "phase", 1)
    alive_mask = (slot_index < counts[0, 0]).astype(jnp.float32)
    mixed = attend(arriving[0, 0], row_document_index[0, 0], alive_mask)
    columns = lax.all_to_all(mixed[None], "dp", split_axis=3, concat_axis=0, tiled=True)
    selected_down_weight = jnp.take(lowrank_down_weight[0], block_adapter_index[0], axis=0)
    project_part = jnp.einsum(
        "psiw,pswr->psir", columns, selected_down_weight, preferred_element_type=jnp.float32
    )
    projected_rows = lax.psum(project_part, "dp")
    scaled_rows = (LOWRANK_SCALE * projected_rows).astype(jnp.bfloat16)
    delta = jnp.einsum(
        "psir,psrw->psiw", scaled_rows, selected_up_weight, preferred_element_type=jnp.float32
    ).astype(jnp.bfloat16)
    backward_scaled_rows = (LOWRANK_SCALE * backward_rows).astype(jnp.bfloat16)
    adapter_indicator = (
        block_adapter_index[0][:, :, None]
        == jnp.arange(lowrank_down_weight.shape[1])[None, None, :]
    ).astype(jnp.float32)
    highest = lax.Precision.HIGHEST
    per_up = jnp.einsum(
        "psir,psiw->psrw", scaled_rows, grad_rows, preferred_element_type=jnp.float32
    )
    grad_up = jnp.einsum("psa,psrw->arw", adapter_indicator, per_up, precision=highest)
    per_down = jnp.einsum(
        "psiw,psir->pswr", columns, backward_scaled_rows, preferred_element_type=jnp.float32
    )
    grad_down = jnp.einsum("psa,pswr->awr", adapter_indicator, per_down, precision=highest)
    return (delta[None], grad_down[None], grad_up[None])


def solution(mesh):
    in_specs = (
        P("phase", "dp", None, None, None),
        P("phase", "dp", None, None),
        P("phase", "dp"),
        P("phase", None, None),
        P("phase", None, "dp", None),
        P("phase", None, None, "dp"),
        P("phase", None, None, None, "dp"),
    )
    out_specs = (
        P("phase", None, None, None, "dp"),
        P("phase", None, "dp", None),
        P("phase", None, None, "dp"),
    )
    return jax.shard_map(
        on_device, mesh=mesh, in_specs=in_specs, out_specs=out_specs, check_vma=False
    )
```

profile of v0, /device:TPU:0, one launch (start us, length us, event | category | flops | bytes accessed | tf_op | source)
XLA Modules:
  0.0 551.2 jit_solution(4620571957671938459)
XLA Ops:
  7.2 0.0 copy-start
  7.2 0.0 copy-start.7
  7.2 8.0 %copy.41 = bf16[1,1,2,128,10240]{3,4,2,1,0:T(8,128)(2,1)} copy(bf16[1,1,2,128,10240]{4,3,2,1,0:T(8,128)(2,1)} %param.7) | data formatting | bytes 10485760 | tf_op args[0]
  15.2 0.0 collective-permute-start
  15.9 0.0 copy-done.7
  15.9 0.1 compare_and_fusion
  16.0 60.2 %collective-permute-done = bf16[1,1,2,128,10240]{3,4,2,1,0:T(8,128)(2,1)S(1)} collective-permute-done((bf16[1,1,2,128,10240]{3,4,2,1,0:T(8,128)(2,1)}, bf16[1,1,2,128,10240]{3,4,2,1,0:T(8,128)(2,1)S(1)}, u32[]{:S(2)}, u32[]{:S(2)}) %collective-permute-start) | collective-permute-done | bytes 5242912 | tf_op jit(solution)/shard_map/ppermute | solution.py:16
  76.2 0.1 fusion.48
  76.3 2.3 slice.18
  78.6 8.4 %fusion.49 = (f32[2,8,8,128]{3,2,1,0:T(8,128)S(1)}, f32[2,8,8,128,128]{3,4,2,1,0:T(8,128)}) fusion(pred[2,128,128]{1,2,0:T(8,128)(4,1)S(1)} %compare_and_fusion, bf16[2,128,8,128,1]{1,3,4,2,0:T(8,128)(2,1)S(1)} %bitcast.85, bf16[2,128,8,8,128]{1,4,3,2,0:T(8,128)(2,1)} %bitcast.82), kind=kOutput, calls=%fused_computation.58 | convolution fusion | flops 545259648 | bytes 13205504 | tf_op jit(solution)/shard_map/sub | solution.py:41
  86.9 7.9 %fusion.16 = f32[2,8,8,128,128]{3,4,2,1,0:T(8,128)} fusion(bf16[2,128,8,128,1]{1,3,4,2,0:T(8,128)(2,1)S(1)} %bitcast.84, f32[2,8,8,128,128]{3,4,2,1,0:T(8,128)} %get-tuple-element.20, f32[2,8,8,128]{3,2,1,0:T(8,128)S(1)} %get-tuple-element.19), kind=kOutput, calls=%fused_computation.23 | convolution fusion | flops 541065216 | bytes 17367040 | tf_op jit(solution)/shard_map/skgij,sjkd->sikgd/dot_general | solution.py:43
  94.8 8.9 %copy.64 = f32[1,2,128,8192]{3,2,1,0:T(8,128)} copy(f32[1,2,128,8192]{2,3,1,0:T(8,128)} %bitcast.79) | data formatting | bytes 16777216 | tf_op jit(solution)/shard_map/reshape | solution.py:44
  103.7 6.1 %multiply_convert_fusion = bf16[1,2,128,8192]{3,2,1,0:T(8,128)(2,1)} fusion(f32[1,2,128,8192]{3,2,1,0:T(8,128)} %copy.64, f32[2]{0:T(128)S(1)} %compare_convert_fusion), kind=kLoop, calls=%fused_computation.4 | loop fusion | flops 4194304 | bytes 12582920 | tf_op jit(solution)/shard_map/convert_element_type | solution.py:45
  109.8 11.1 %copy.46 = bf16[1,2,128,8192]{2,1,0,3:T(2,128)(2,1)} copy(bf16[1,2,128,8192]{3,2,1,0:T(8,128)(2,1)} %multiply_convert_fusion) | data formatting | bytes 8388608 | tf_op jit(solution)/shard_map/convert_element_type | solution.py:45
  121.0 0.0 copy-start.6
  121.0 8.9 %all-to-all-start = ((bf16[1,2,128,8192]{2,1,0,3:T(2,128)(2,1)}), bf16[1,2,128,8192]{2,1,0,3:T(2,128)(2,1)}, u32[]{:S(2)}, u32[]{:S(2)}) async-start(bf16[1,2,128,8192]{2,1,0,3:T(2,128)(2,1)} %copy.46), calls=%async_computation | async-start | bytes 8388608 | tf_op jit(solution)/shard_map/all_to_all | solution.py:67
  129.8 0.0 all-reduce.3.cloned.1.call-start
  129.9 0.0 copy-done.6
  129.9 0.1 copy.49
  130.0 0.1 copy.50
  130.1 0.1 reshape.98
  130.2 0.0 copy-done
  130.2 0.7 gather_fusion
  130.9 3.2 gather_fusion.1
  134.2 5.8 %fusion.26 = f32[32,2,128,64]{2,3,1,0:T(8,128)} fusion(bf16[1,32,2,128,256]{4,3,2,1,0:T(8,128)(2,1)} %param.13, bf16[32,2,64,256]{3,2,1,0:T(8,128)(2,1)} %bitcast.77, pred[32,2]{1,0:T(8,128)(4,1)S(1)} %copy.49), kind=kOutput, calls=%fused_computation.32 | convolution fusion | flops 269484032 | bytes 8388672 | tf_op jit(solution)/shard_map/psiw,psrw->psir/dot_general | solution.py:60
  139.9 45.8 %all-to-all-done = bf16[1,2,128,8192]{2,1,0,3:T(2,128)(2,1)} async-done(((bf16[1,2,128,8192]{2,1,0,3:T(2,128)(2,1)}), bf16[1,2,128,8192]{2,1,0,3:T(2,128)(2,1)}, u32[]{:S(2)}, u32[]{:S(2)}) %all-to-all-start) | async-done | bytes 4194336 | tf_op jit(solution)/shard_map/all_to_all | solution.py:67
  185.8 10.9 %copy.48 = bf16[1,2,128,32,256]{4,2,1,3,0:T(8,128)(2,1)} copy(bf16[1,2,128,32,256]{2,1,4,3,0:T(2,128)(2,1)} %bitcast.12) | data formatting | bytes 8388608 | tf_op jit(solution)/shard_map/all_to_all | solution.py:67
  196.7 5.1 fusion.8
  201.8 0.0 copy-start.2
  201.8 0.0 all-reduce.3.cloned.1.call-update
  201.8 320.3 %all-reduce.3.cloned.1.call-done = (f32[32,2,128,64]{2,3,1,0:T(8,128)}, f32[32,2,128,64]{2,3,1,0:T(8,128)}) async-done(((f32[32,2,128,64]{2,3,1,0:T(8,128)}, f32[32,2,128,64]{2,3,1,0:T(8,128)}), (f32[32,2,128,64]{2,3,1,0:T(8,128)}, f32[32,2,128,64]{2,3,1,0:T(8,128)})) %all-reduce.3.cloned.1.call-update) | async-done | bytes 4194320 | tf_op jit(solution)/shard_map/psum | solution.py:72
  522.2 0.0 copy-done.2
  522.2 0.0 copy-start.3
  522.2 0.0 copy-start.4
  522.2 5.1 convert_bitcast_fusion
  527.2 0.0 copy-done.3
  527.2 0.0 copy-done.4
  527.2 0.0 copy-start.1
  527.2 0.0 copy-start.5
  527.3 0.7 fusion.2
  528.0 1.5 copy-done.1
  529.4 0.7 copy-done.5
  530.1 0.7 fusion.6
  530.8 4.1 fusion.20
  534.9 2.5 copy.54
  537.5 4.3 fusion.23
  541.8 2.5 copy.55
  (5 shorter events, 0.0 us)
Async XLA Ops:
  7.2 123.1 %copy-start = (bf16[1,32,256,64]{2,3,1,0:T(8,128)(2,1)S(1)}, bf16[1,32,256,64]{2,3,1,0:T(8,128)(2,1)}, u32[]{:S(2)}) copy-start(bf16[1,32,256,64]{2,3,1,0:T(8,128)(2,1)} %param.11) | copy-start | bytes 3145732
  7.2 8.7 %copy-start.7 = (s32[1,1,2,128]{3,2,1,0:T(2,128)S(1)}, s32[1,1,2,128]{3,2,1,0:T(2,128)}, u32[]{:S(2)}) copy-start(s32[1,1,2,128]{3,2,1,0:T(2,128)} %param.8) | copy-start | bytes 3076
  15.2 61.0 %collective-permute-start = (bf16[1,1,2,128,10240]{3,4,2,1,0:T(8,128)(2,1)}, bf16[1,1,2,128,10240]{3,4,2,1,0:T(8,128)(2,1)S(1)}, u32[]{:S(2)}, u32[]{:S(2)}) collective-permute-start(bf16[1,1,2,128,10240]{3,4,2,1,0:T(8,128)(2,1)} %copy.41), channel_id=1, source_target_pairs={{0,32},{32,64},{64,96},{96,0},{1,33},{33,65},{65,97},{97,1},{2,34}... | collective-permute-start | bytes 15728648 | tf_op jit(solution)/shard_map/ppermute | solution.py:16
  121.0 8.9 %copy-start.6 = (s32[1,32,2]{1,2,0:T(2,128)S(1)}, s32[1,32,2]{1,2,0:T(2,128)}, u32[]{:S(2)}) copy-start(s32[1,32,2]{1,2,0:T(2,128)} %param.10) | copy-start | bytes 772
  121.0 64.8 %all-to-all-start = ((bf16[1,2,128,8192]{2,1,0,3:T(2,128)(2,1)}), bf16[1,2,128,8192]{2,1,0,3:T(2,128)(2,1)}, u32[]{:S(2)}, u32[]{:S(2)}) async-start(bf16[1,2,128,8192]{2,1,0,3:T(2,128)(2,1)} %copy.46), calls=%async_computation | async-start | bytes 8388608 | tf_op jit(solution)/shard_map/all_to_all | solution.py:67
  129.8 392.3 %all-reduce.3.cloned.1.call-start = ((), (), s32[]{:S(2)}) async-start(), calls=%async_computation.1 | async-start | bytes 8388608 | tf_op jit(solution)/shard_map/psum | solution.py:72
  201.8 320.4 %copy-start.2 = (bf16[64,64,256]{2,1,0:T(8,128)(2,1)S(1)}, bf16[64,64,256]{2,1,0:T(8,128)(2,1)}, u32[]{:S(2)}) copy-start(bf16[64,64,256]{2,1,0:T(8,128)(2,1)} %gather_fusion.1) | copy-start | bytes 6291460
  522.2 5.1 copy-start.3
  522.2 5.1 copy-start.4
  527.2 2.2 copy-start.1
  527.2 2.9 copy-start.5
Sparse Core Ops, SparseCore 0:
  202.0 320.1 all-reduce.2
where the time goes:
time: 552 us; the launch traced here: 551 us
  waiting for transfers between devices  426 us (77%)
  local copies, waits for them, and re-layouts  52.8 us (10%)
  matrix products  42 us (8%)
  between operations  14.8 us (3%)
  starting transfers between devices  8.91 us (2%)
  other arithmetic  6.25 us (1%)
    psum x1, waiting for transfers between devices, on_device(): projected_rows = lax.psum(project_part, 'dp')  320 us
    ppermute x1, waiting for transfers between devices, shifted(): lax.ppermute(array, axis, [(i, (i + by) % peers) for i in range(peers)])  60.2 us
    all_to_all x1, waiting for transfers between devices, on_device(): lax.all_to_all(mixed[None], 'dp', split_axis=3, concat_axis=0, tiled=True)  45.8 us
    unnamed x19, local copies, waits for them, and re-layouts  15.2 us
    convert_element_type x1, local copies, waits for them, and re-layouts, attend(): return (mixed * alive_mask[:, None, None]).astype(jnp.bfloat16)  11.1 us
  transfers between devices with their start and end apart: 3, of which 3 were waited for; matrix products, arithmetic and copies ran while one was open for 2% of the time, Pallas kernels for 0%

commit v1 on v0

v1 whole, which is shorter than its diff:
```python
import math

import jax
import jax.numpy as jnp
from jax import lax
from jax.experimental import pallas as pl
from jax.experimental.pallas import tpu as pltpu
from jax.sharding import PartitionSpec as P

HEADS = 64
KV_HEADS = 8
HEAD_DIM = 128
GROUP = HEADS // KV_HEADS
WIDTH = HEADS * HEAD_DIM
RANK = 64
ROWS = 128
SLOTS = 2
SECTIONS = 4
BINS = 32
BLOCKS = BINS * SLOTS
SHARD = WIDTH // BINS
ADAPTERS = 32
LOWRANK_SCALE = 2.0
C_CHUNKS = 4
G_EARLY = 16
MESH = pl.DeviceIdType.MESH
F32 = jnp.float32
BF16 = jnp.bfloat16


def dot(a, b, ca, cb):
    return lax.dot_general(
        a, b, (((ca,), (cb,)), ((), ())), preferred_element_type=F32
    )


def partner(me, step):
    kz, kx = step // 16, step % 4
    ky = ((step // 4) % 4 + 4 - kx) % 4
    x, y, z = me // 8, (me // 2) % 4, me % 2
    return ((x + kx) % 4) * 8 + ((y + ky) % 4) * 2 + (z + kz) % 2


def owner_kernel(
    index_ref, info_ref, up_ref, down_ref, cot_hbm, qkv_hbm,
    scaled_out, grad_out,
    cot, qkv, info_in, bias, back_send, back_recv, down_send, down_recv, mixed, scaled, grad_send,
    cot_sem, qkv_sem, info_sem, back_sem, down_sem, scaled_sem, grad_sem,
):
    phase, me = lax.axis_index("phase"), lax.axis_index("dp")
    owners, shards = (phase + SECTIONS - 1) % SECTIONS, (phase + 1) % SECTIONS

    def remote(src, dst, sem, section, to):
        return pltpu.make_async_remote_copy(
            src_ref=src, dst_ref=dst, send_sem=sem.at[0], recv_sem=sem.at[1],
            device_id=(section, to), device_id_type=MESH,
        )

    per_chunk = BLOCKS // C_CHUNKS

    def cot_copy(chunk):
        at = pl.ds(chunk * per_chunk, per_chunk)
        return pltpu.make_async_copy(cot_hbm.at[at], cot.at[at], cot_sem.at[chunk])

    for chunk in range(C_CHUNKS):
        cot_copy(chunk).start()
    qkv_copy = pltpu.make_async_copy(qkv_hbm, qkv, qkv_sem)
    qkv_copy.start()

    barrier = pltpu.get_barrier_semaphore()

    def greet(step, _):
        pl.semaphore_signal(
            barrier, inc=1, device_id=(shards, partner(me, step)), device_id_type=MESH
        )
        return 0

    lax.fori_loop(0, BINS, greet, 0)

    for chunk in range(C_CHUNKS):
        cot_copy(chunk).wait()

        def back_part(owner, _):
            for slot in range(SLOTS):
                up = up_ref[index_ref[slot, owner]]
                part = dot(up, cot[owner * SLOTS + slot], 1, 1)
                back_send[owner, :, slot * ROWS : (slot + 1) * ROWS] = part.astype(BF16)
            return 0

        lax.fori_loop(
            chunk * per_chunk // SLOTS, (chunk + 1) * per_chunk // SLOTS, back_part, 0
        )

    pl.semaphore_wait(barrier, BINS)
    info_copy = remote(info_ref, info_in, info_sem, owners, me)
    info_copy.start()

    def send_back(step, _):
        to = partner(me, step)
        remote(back_send.at[to], back_recv.at[me], back_sem, owners, to).start()
        return 0

    lax.fori_loop(0, BINS, send_back, 0)

    def send_down(step, _):
        to = partner(me, step)
        for slot in range(SLOTS):
            down_send[to, slot * RANK : (slot + 1) * RANK] = down_ref[index_ref[slot, to]]
        remote(down_send.at[to], down_recv.at[me], down_sem, owners, to).start()
        return 0

    lax.fori_loop(0, BINS, send_down, 0)

    info_copy.wait()
    row = lax.broadcasted_iota(jnp.int32, (ROWS, ROWS), 0)
    column = lax.broadcasted_iota(jnp.int32, (ROWS, ROWS), 1)
    for slot in range(SLOTS):
        documents = jnp.broadcast_to(info_in[slot : slot + 1, :].astype(F32), (ROWS, ROWS))
        kept = (documents == documents.T) & (column <= row)
        bias[slot] = jnp.where(kept, 0.0, -1e30)
    qkv_copy.wait()
    to_power_of_two = math.log2(math.e) * HEAD_DIM**-0.5

    def attend(step, _):
        slot, kv = step // KV_HEADS, step % KV_HEADS
        alive = jnp.where(info_in[SLOTS : SLOTS + 1, :] > slot, 1.0, 0.0)
        keys = qkv[slot, :, pl.ds(pl.multiple_of(WIDTH + kv * HEAD_DIM, HEAD_DIM), HEAD_DIM)]
        values = qkv[
            slot, :, pl.ds(pl.multiple_of(WIDTH + (KV_HEADS + kv) * HEAD_DIM, HEAD_DIM), HEAD_DIM)
        ]
        values_and_ones = jnp.concatenate([values, jnp.ones_like(values)], axis=1)
        for head in range(GROUP):
            at = pl.ds(pl.multiple_of((kv * GROUP + head) * HEAD_DIM, HEAD_DIM), HEAD_DIM)
            scores = dot(qkv[slot, :, at], keys, 1, 1) + bias[slot]
            top = jnp.max(scores, axis=-1, keepdims=True)
            powers = jnp.exp2((scores - top) * to_power_of_two).astype(BF16)
            both = dot(powers, values_and_ones, 1, 0)
            mixed[slot, :, at] = (
                both[:, :HEAD_DIM] * (alive / both[:, HEAD_DIM:])
            ).astype(BF16)
        return 0

    lax.fori_loop(0, SLOTS * KV_HEADS, attend, 0)

    remote(back_send, back_recv, back_sem, owners, me).wait_recv()

    def add_back(source, total):
        return total + back_recv[source].astype(F32)

    back = lax.fori_loop(0, BINS, add_back, jnp.zeros((RANK, SLOTS * ROWS), F32))
    back_scaled = (LOWRANK_SCALE * back).astype(BF16)

    def send_grad(step, _):
        to = partner(me, step)
        at = pl.ds(pl.multiple_of(to * SHARD, SHARD), SHARD)
        for slot in range(SLOTS):
            part = dot(back_scaled[:, slot * ROWS : (slot + 1) * ROWS], mixed[slot, :, at], 1, 0)
            grad_send[to, slot * RANK : (slot + 1) * RANK] = part.astype(BF16)
        remote(grad_send.at[to], grad_out.at[me], grad_sem, shards, to).start()
        return 0

    def project(source, totals):
        at = pl.ds(pl.multiple_of(source * SHARD, SHARD), SHARD)
        return tuple(
            totals[slot]
            + dot(down_recv[source, slot * RANK : (slot + 1) * RANK], mixed[slot, :, at], 1, 1)
            for slot in range(SLOTS)
        )

    lax.fori_loop(0, G_EARLY, send_grad, 0)
    remote(down_send, down_recv, down_sem, owners, me).wait_recv()
    projected = lax.fori_loop(
        0, BINS, project, tuple(jnp.zeros((RANK, ROWS), F32) for _ in range(SLOTS))
    )
    for slot in range(SLOTS):
        scaled[:, slot * ROWS : (slot + 1) * ROWS] = (LOWRANK_SCALE * projected[slot]).astype(BF16)

    def send_scaled(step, _):
        to = partner(me, step)
        remote(scaled, scaled_out.at[me], scaled_sem, shards, to).start()
        return 0

    lax.fori_loop(0, BINS, send_scaled, 0)
    lax.fori_loop(G_EARLY, BINS, send_grad, 0)

    remote(back_send, back_recv, back_sem, owners, me).wait_send()
    remote(down_send, down_recv, down_sem, owners, me).wait_send()
    whole_grad = remote(grad_send, grad_out, grad_sem, shards, me)
    whole_scaled = remote(back_send, scaled_out, scaled_sem, shards, me)
    whole_scaled.wait_recv()
    whole_scaled.wait_send()
    whole_grad.wait_recv()
    whole_grad.wait_send()


def owner_call(index, info, up, down, cotangent, qkv):
    vmem, hbm = pl.BlockSpec(memory_space=pltpu.VMEM), pl.BlockSpec(memory_space=pl.ANY)
    return pl.pallas_call(
        owner_kernel,
        out_shape=(
            jax.ShapeDtypeStruct((BINS, RANK, SLOTS * ROWS), BF16),
            jax.ShapeDtypeStruct((BINS, SLOTS * RANK, SHARD), BF16),
        ),
        in_specs=[pl.BlockSpec(memory_space=pltpu.SMEM), vmem, vmem, vmem, hbm, hbm],
        out_specs=(hbm, hbm),
        scratch_shapes=[
            pltpu.VMEM((BLOCKS, ROWS, SHARD), BF16),
            pltpu.VMEM(qkv.shape, BF16),
            pltpu.VMEM((8, ROWS), jnp.int32),
            pltpu.VMEM((SLOTS, ROWS, ROWS), F32),
            pltpu.VMEM((BINS, RANK, SLOTS * ROWS), BF16),
            pltpu.VMEM((BINS, RANK, SLOTS * ROWS), BF16),
            pltpu.VMEM((BINS, SLOTS * RANK, SHARD), BF16),
            pltpu.VMEM((BINS, SLOTS * RANK, SHARD), BF16),
            pltpu.VMEM((SLOTS, ROWS, WIDTH), BF16),
            pltpu.VMEM((RANK, SLOTS * ROWS), BF16),
            pltpu.VMEM((BINS, SLOTS * RANK, SHARD), BF16),
            pltpu.SemaphoreType.DMA((C_CHUNKS,)),
            pltpu.SemaphoreType.DMA,
            pltpu.SemaphoreType.DMA((2,)),
            pltpu.SemaphoreType.DMA((2,)),
            pltpu.SemaphoreType.DMA((2,)),
            pltpu.SemaphoreType.DMA((2,)),
            pltpu.SemaphoreType.DMA((2,)),
        ],
        compiler_params=pltpu.CompilerParams(
            collective_id=0, has_side_effects=True, vmem_limit_bytes=48 << 20
        ),
        name="owner",
    )(index, info, up, down, cotangent, qkv)


STEP_BLOCKS = 8


def shard_kernel(index_ref, scaled_ref, grad_ref, cot_ref, up_ref, delta_ref, down_out, up_out):
    step = pl.program_id(0)

    @pl.when(step == 0)
    def _():
        down_out[...] = jnp.zeros_like(down_out)
        up_out[...] = jnp.zeros_like(up_out)

    for at in range(STEP_BLOCKS):
        bin_at, slot = at // SLOTS, at % SLOTS
        adapter = index_ref[slot, step * (STEP_BLOCKS // SLOTS) + bin_at]
        scaled = scaled_ref[bin_at, :, slot * ROWS : (slot + 1) * ROWS]
        delta_ref[at] = dot(scaled, up_ref[adapter], 0, 0).astype(BF16)
        up_out[adapter] += dot(scaled, cot_ref[at], 1, 0)
        down_out[adapter] += grad_ref[bin_at, slot * RANK : (slot + 1) * RANK].astype(F32)


def shard_call(index, scaled, grad, cotangent, up):
    bins = STEP_BLOCKS // SLOTS
    whole = pl.BlockSpec((ADAPTERS, RANK, SHARD), lambda i, _: (0, 0, 0))
    return pl.pallas_call(
        shard_kernel,
        out_shape=(
            jax.ShapeDtypeStruct((BLOCKS, ROWS, SHARD), BF16),
            jax.ShapeDtypeStruct((ADAPTERS, RANK, SHARD), F32),
            jax.ShapeDtypeStruct((ADAPTERS, RANK, SHARD), F32),
        ),
        grid_spec=pltpu.PrefetchScalarGridSpec(
            num_scalar_prefetch=1,
            grid=(BLOCKS // STEP_BLOCKS,),
            in_specs=[
                pl.BlockSpec((bins, RANK, SLOTS * ROWS), lambda i, _: (i, 0, 0)),
                pl.BlockSpec((bins, SLOTS * RANK, SHARD), lambda i, _: (i, 0, 0)),
                pl.BlockSpec((STEP_BLOCKS, ROWS, SHARD), lambda i, _: (i, 0, 0)),
                whole,
            ],
            out_specs=(
                pl.BlockSpec((STEP_BLOCKS, ROWS, SHARD), lambda i, _: (i, 0, 0)),
                whole,
                whole,
            ),
        ),
        compiler_params=pltpu.CompilerParams(vmem_limit_bytes=40 << 20),
        name="shard",
    )(index, scaled, grad, cotangent, up)


def on_device(
    query_key_value_blocks,
    row_document_index,
    counts,
    block_adapter_index,
    lowrank_down_weight,
    lowrank_up_weight,
    cotangent,
):
    index = block_adapter_index[0].T
    info = jnp.concatenate(
        [
            row_document_index[0, 0],
            jnp.broadcast_to(counts, (8 - SLOTS, ROWS)),
        ]
    )
    up = lowrank_up_weight[0]
    down = lowrank_down_weight[0].transpose(0, 2, 1)
    cot = cotangent.reshape(BLOCKS, ROWS, SHARD)
    scaled, grad = owner_call(index, info, up, down, cot, query_key_value_blocks[0, 0])
    delta, grad_down, grad_up = shard_call(index, scaled, grad, cot, up)
    return (
        delta.reshape(cotangent.shape),
        grad_down.transpose(0, 2, 1)[None],
        grad_up[None],
    )


def solution(mesh):
    in_specs = (
        P("phase", "dp", None, None, None),
        P("phase", "dp", None, None),
        P("phase", "dp"),
        P("phase", None, None),
        P("phase", None, "dp", None),
        P("phase", None, None, "dp"),
        P("phase", None, None, None, "dp"),
    )
    out_specs = (
        P("phase", None, None, None, "dp"),
        P("phase", None, "dp", None),
        P("phase", None, None, "dp"),
    )
    return jax.shard_map(
        on_device, mesh=mesh, in_specs=in_specs, out_specs=out_specs, check_vma=False
    )
```

time: 552 us -> 101 us (0.18)
  the two profiles are of different devices: /device:TPU:0 before, /device:TPU:1 now
where the time goes in v1:
time: 101 us
  Pallas kernels  95.8 us (95%)
  local copies, waits for them, and re-layouts  3.82 us (4%)
  between operations  1.3 us (1%)
    pallas_call x1, Pallas kernels, owner_call(): pl.pallas_call(owner_kernel, out_shape=(jax.ShapeDtypeStruct((BINS, RANK,...  88.5 us
    pallas_call x1, Pallas kernels, shard_call(): pl.pallas_call(shard_kernel, out_shape=(jax.ShapeDtypeStruct((BLOCKS, ROW...  7.37 us
    unnamed x8, local copies, waits for them, and re-layouts  3.13 us

profile of v1, /device:TPU:1, one launch (start us, length us, event | category | flops | bytes accessed | tf_op | source)
XLA Modules:
  0.0 100.9 jit_solution(14249786426851315471)
XLA Ops:
  1.3 0.7 concatenate.3.info_ref
  2.0 0.0 copy-start.1
  2.0 1.2 %copy-done.1 = bf16[1,32,64,256]{3,2,1,0:T(8,128)(2,1)S(1)} copy-done((bf16[1,32,64,256]{3,2,1,0:T(8,128)(2,1)S(1)}, bf16[1,32,64,256]{3,2,1,0:T(8,128)(2,1)}, u32[]{:S(2)}) %copy-start.1) | copy-done | bytes 1048600
  3.2 0.0 copy-start.2
  3.2 1.2 %copy-done.2 = bf16[1,32,256,64]{2,3,1,0:T(8,128)(2,1)S(1)} copy-done((bf16[1,32,256,64]{2,3,1,0:T(8,128)(2,1)S(1)}, bf16[1,32,256,64]{2,3,1,0:T(8,128)(2,1)}, u32[]{:S(2)}) %copy-start.2) | copy-done | bytes 1048600
  4.4 0.0 copy-start.3
  4.4 0.7 copy-done.3
  5.1 0.0 copy-start
  5.1 88.5 %owner.1 = (bf16[32,64,256]{2,1,0:T(8,128)(2,1)S(1)}, bf16[32,128,256]{2,1,0:T(8,128)(2,1)S(1)}) custom-call(s32[2,32]{1,0:T(2,128)S(1)} %bitcast.22, s32[8,128]{1,0:T(8,128)S(1)} %concatenate.3.info_ref, bf16[32,64,256]{2,1,0:T(8,128)(2,1)S(1)} %bitcast.19, bf16[32,64,256]{2,1,0:T(8,128)(2,1)S(1)} %bitcast.21, bf16[64,128,256]{2,1,0:T(8,128)(2,1)} %bitcast.17, ...), custom_call_target="tpu_custom_call" | custom-call | tf_op jit(solution)/shard_map/owner/pallas_call | solution.py:198
  93.6 0.0 copy-done
  93.6 7.4 %shard.1 = (bf16[64,128,256]{2,1,0:T(8,128)(2,1)}, f32[32,64,256]{2,1,0:T(8,128)}, f32[32,64,256]{2,1,0:T(8,128)}) custom-call(s32[2,32]{1,0:T(2,128)S(1)} %bitcast.23, bf16[32,64,256]{2,1,0:T(8,128)(2,1)S(1)} %get-tuple-element.8.scaled_ref, bf16[32,128,256]{2,1,0:T(8,128)(2,1)S(1)} %get-tuple-element.9.grad_ref, bf16[64,128,256]{2,1,0:T(8,128)(2,1)S(1)} %bitcast.18, ...), custom_call_target="tpu_custom_call" | custom-call | tf_op jit(solution)/shard_map/shard/pallas_call | solution.py:256
Async XLA Ops:
  2.0 1.2 %copy-start.1 = (bf16[1,32,64,256]{3,2,1,0:T(8,128)(2,1)S(1)}, bf16[1,32,64,256]{3,2,1,0:T(8,128)(2,1)}, u32[]{:S(2)}) copy-start(bf16[1,32,64,256]{3,2,1,0:T(8,128)(2,1)} %param.12) | copy-start | bytes 3145732
  3.2 1.2 %copy-start.2 = (bf16[1,32,256,64]{2,3,1,0:T(8,128)(2,1)S(1)}, bf16[1,32,256,64]{2,3,1,0:T(8,128)(2,1)}, u32[]{:S(2)}) copy-start(bf16[1,32,256,64]{2,3,1,0:T(8,128)(2,1)} %param.11) | copy-start | bytes 3145732
  4.4 0.7 copy-start.3
  5.1 88.5 %copy-start = (bf16[1,32,2,128,256]{4,3,2,1,0:T(8,128)(2,1)S(1)}, bf16[1,32,2,128,256]{4,3,2,1,0:T(8,128)(2,1)}, u32[]{:S(2)}) copy-start(bf16[1,32,2,128,256]{4,3,2,1,0:T(8,128)(2,1)} %param.13) | copy-start | bytes 12582916

commit v2 on v1

v2 whole, which is shorter than its diff:
```python
import math

import jax
import jax.numpy as jnp
from jax import lax
from jax.experimental import pallas as pl
from jax.experimental.pallas import tpu as pltpu
from jax.sharding import PartitionSpec as P

HEADS = 64
KV_HEADS = 8
HEAD_DIM = 128
GROUP = HEADS // KV_HEADS
WIDTH = HEADS * HEAD_DIM
RANK = 64
ROWS = 128
SLOTS = 2
SECTIONS = 4
BINS = 32
BLOCKS = BINS * SLOTS
SHARD = WIDTH // BINS
ADAPTERS = 32
LOWRANK_SCALE = 2.0
MESH = pl.DeviceIdType.MESH
F32 = jnp.float32
BF16 = jnp.bfloat16


def hold(array):
    return pltpu.with_memory_space_constraint(array, pltpu.HBM)


def dot(a, b, ca, cb):
    return lax.dot_general(
        a, b, (((ca,), (cb,)), ((), ())), preferred_element_type=F32
    )


def partner(me, step):
    kx, turn = step % 4, (step // 4) % 4
    ky, kz = (turn + 4 - kx) % 4, (step // 16 + turn + kx) % 2
    x, y, z = me // 8, (me // 2) % 4, me % 2
    return ((x + kx) % 4) * 8 + ((y + ky) % 4) * 2 + (z + kz) % 2


def owner_kernel(
    index_hbm, documents_hbm, counts_hbm, up_hbm, down_hbm, cot_hbm, qkv_hbm,
    grad_out, delta_out, per_up_out,
    index_ref, counts_ref, up_ref, down_ref, cot, qkv, documents_own, info_own, info_in, bias,
    back_send, back_recv, down_send, down_recv, mixed, scaled, scaled_in, grad_send,
    load_sem, info_sem, back_sem, down_sem, scaled_sem, grad_sem,
):
    phase, me = lax.axis_index("phase"), lax.axis_index("dp")
    owners, shards = (phase + SECTIONS - 1) % SECTIONS, (phase + 1) % SECTIONS

    def remote(src, dst, sem, section, to):
        return pltpu.make_async_remote_copy(
            src_ref=src, dst_ref=dst, send_sem=sem.at[0], recv_sem=sem.at[1],
            device_id=(section, to), device_id_type=MESH,
        )

    loads = [
        pltpu.make_async_copy(src, dst, load_sem.at[i])
        for i, (src, dst) in enumerate(
            (
                (index_hbm, index_ref),
                (counts_hbm, counts_ref),
                (documents_hbm, documents_own),
                (down_hbm, down_ref),
                (up_hbm, up_ref),
                (cot_hbm, cot),
                (qkv_hbm, qkv),
            )
        )
    ]
    for load in loads:
        load.start()
    index_load, counts_load, documents_load, down_load, up_load, cot_load, qkv_load = loads

    barrier = pltpu.get_barrier_semaphore()

    def greet(step, _):
        pl.semaphore_signal(
            barrier, inc=1, device_id=(shards, partner(me, step)), device_id_type=MESH
        )
        return 0

    lax.fori_loop(0, BINS, greet, 0)

    counts_load.wait()
    documents_load.wait()
    info_own[...] = jnp.full(info_own.shape, counts_ref[0, 0], jnp.int32)
    info_own[:SLOTS] = documents_own[...]
    index_load.wait()
    down_load.wait()

    def choose_down(to, _):
        for slot in range(SLOTS):
            down_send[to, slot * RANK : (slot + 1) * RANK] = down_ref[index_ref[slot, to]]
        return 0

    lax.fori_loop(0, BINS, choose_down, 0, unroll=4)

    pl.semaphore_wait(barrier, BINS)
    info_copy = remote(info_own, info_in, info_sem, owners, me)
    info_copy.start()

    def send_down(step, _):
        to = partner(me, step)
        remote(down_send.at[to], down_recv.at[me], down_sem, owners, to).start()
        return 0


    up_load.wait()
    cot_load.wait()

    def send_back(step, _):
        to = partner(me, step)
        for slot in range(SLOTS):
            part = dot(up_ref[index_ref[slot, to]], cot[to * SLOTS + slot], 1, 1)
            back_send[to, :, slot * ROWS : (slot + 1) * ROWS] = part.astype(BF16)
        remote(back_send.at[to], back_recv.at[me], back_sem, owners, to).start()
        return 0

    lax.fori_loop(0, BINS, send_back, 0, unroll=4)

    lax.fori_loop(0, BINS, send_down, 0)

    info_copy.wait()
    row = lax.broadcasted_iota(jnp.int32, (ROWS, ROWS), 0)
    column = lax.broadcasted_iota(jnp.int32, (ROWS, ROWS), 1)
    for slot in range(SLOTS):
        documents = jnp.broadcast_to(info_in[slot : slot + 1, :].astype(F32), (ROWS, ROWS))
        kept = (documents == documents.T) & (column <= row)
        bias[slot] = jnp.where(kept, 0.0, -1e30)
    qkv_load.wait()
    to_power_of_two = math.log2(math.e) * HEAD_DIM**-0.5

    def attend(step, _):
        slot, kv = step // KV_HEADS, step % KV_HEADS
        alive = jnp.where(info_in[SLOTS : SLOTS + 1, :] > slot, 1.0, 0.0)
        keys = qkv[slot, :, pl.ds(pl.multiple_of(WIDTH + kv * HEAD_DIM, HEAD_DIM), HEAD_DIM)]
        values = qkv[
            slot, :, pl.ds(pl.multiple_of(WIDTH + (KV_HEADS + kv) * HEAD_DIM, HEAD_DIM), HEAD_DIM)
        ]
        heads = [
            pl.ds(pl.multiple_of((kv * GROUP + head) * HEAD_DIM, HEAD_DIM), HEAD_DIM)
            for head in range(GROUP)
        ]
        queries = jnp.concatenate([qkv[slot, :, at] for at in heads], axis=0)
        scores = dot(queries, keys, 1, 1).reshape(GROUP, ROWS, ROWS) + bias[slot]
        top = jnp.max(scores, axis=-1, keepdims=True)
        powers = jnp.exp2((scores - top) * to_power_of_two)
        weights = powers * (1.0 / jnp.sum(powers, axis=-1, keepdims=True))
        weights = weights.astype(BF16).reshape(GROUP * ROWS, ROWS)
        group = (dot(weights, values, 1, 0) * alive).astype(BF16)
        for head, at in enumerate(heads):
            mixed[slot, :, at] = group[head * ROWS : (head + 1) * ROWS]
        return 0

    lax.fori_loop(0, SLOTS * KV_HEADS, attend, 0, unroll=2)

    def piece(which):
        at = pl.ds(pl.multiple_of(which * SHARD, SHARD), SHARD)
        return mixed[:, :, at].reshape(SLOTS * ROWS, SHARD)

    def project(source, total):
        return total + dot(down_recv[source], piece(source), 1, 1)

    remote(down_send, down_recv, down_sem, owners, me).wait_recv()
    projected = lax.fori_loop(
        0, BINS, project, jnp.zeros((SLOTS * RANK, SLOTS * ROWS), F32), unroll=4
    )
    for slot in range(SLOTS):
        at = slice(slot * ROWS, (slot + 1) * ROWS)
        own = projected[slot * RANK : (slot + 1) * RANK, at]
        scaled[:, at] = (LOWRANK_SCALE * own).astype(BF16)

    def send_scaled(step, _):
        to = partner(me, step)
        remote(scaled, scaled_in.at[me], scaled_sem, shards, to).start()
        return 0

    lax.fori_loop(0, BINS, send_scaled, 0)

    remote(back_send, back_recv, back_sem, owners, me).wait_recv()

    def add_back(source, total):
        return total + back_recv[source].astype(F32)

    back = lax.fori_loop(0, BINS, add_back, jnp.zeros((RANK, SLOTS * ROWS), F32), unroll=4)
    back_scaled = (LOWRANK_SCALE * back).astype(BF16)
    nothing = jnp.zeros((RANK, ROWS), BF16)
    back_diagonal = jnp.concatenate(
        [
            jnp.concatenate([back_scaled[:, :ROWS], nothing], axis=1),
            jnp.concatenate([nothing, back_scaled[:, ROWS:]], axis=1),
        ],
        axis=0,
    )

    def send_grad(step, _):
        to = partner(me, step)
        grad_send[to] = dot(back_diagonal, piece(to), 1, 0).astype(BF16)
        remote(grad_send.at[to], grad_out.at[me], grad_sem, shards, to).start()
        return 0

    lax.fori_loop(0, BINS, send_grad, 0, unroll=4)

    whole_scaled = remote(back_send, scaled_in, scaled_sem, shards, me)
    whole_scaled.wait_recv()

    def spread(source, _):
        for slot in range(SLOTS):
            block = source * SLOTS + slot
            own = scaled_in[source, :, slot * ROWS : (slot + 1) * ROWS]
            delta_out[block] = dot(own, up_ref[index_ref[slot, source]], 0, 0).astype(BF16)
            per_up_out[block] = dot(own, cot[block], 1, 0)
        return 0

    lax.fori_loop(0, BINS, spread, 0, unroll=2)

    remote(back_send, back_recv, back_sem, owners, me).wait_send()
    remote(down_send, down_recv, down_sem, owners, me).wait_send()
    whole_scaled.wait_send()
    whole_grad = remote(grad_send, grad_out, grad_sem, shards, me)
    whole_grad.wait_recv()
    whole_grad.wait_send()


def owner_call(index, documents, counts, up, down, cotangent, qkv):
    vmem, hbm = pl.BlockSpec(memory_space=pltpu.VMEM), pl.BlockSpec(memory_space=pl.ANY)
    return pl.pallas_call(
        owner_kernel,
        out_shape=(
            jax.ShapeDtypeStruct((BINS, SLOTS * RANK, SHARD), BF16),
            jax.ShapeDtypeStruct((BLOCKS, ROWS, SHARD), BF16),
            jax.ShapeDtypeStruct((BLOCKS, RANK, SHARD), F32),
        ),
        in_specs=[pl.BlockSpec(memory_space=pltpu.HBM)] * 7,
        out_specs=(hbm, vmem, vmem),
        scratch_shapes=[
            pltpu.SMEM((SLOTS, BINS), jnp.int32),
            pltpu.SMEM((1, 1), jnp.int32),
            pltpu.VMEM((ADAPTERS, RANK, SHARD), BF16),
            pltpu.VMEM((ADAPTERS, RANK, SHARD), BF16),
            pltpu.VMEM((BLOCKS, ROWS, SHARD), BF16),
            pltpu.VMEM(qkv.shape, BF16),
            pltpu.VMEM((SLOTS, ROWS), jnp.int32),
            pltpu.VMEM((8, ROWS), jnp.int32),
            pltpu.VMEM((8, ROWS), jnp.int32),
            pltpu.VMEM((SLOTS, ROWS, ROWS), F32),
            pltpu.VMEM((BINS, RANK, SLOTS * ROWS), BF16),
            pltpu.VMEM((BINS, RANK, SLOTS * ROWS), BF16),
            pltpu.VMEM((BINS, SLOTS * RANK, SHARD), BF16),
            pltpu.VMEM((BINS, SLOTS * RANK, SHARD), BF16),
            pltpu.VMEM((SLOTS, ROWS, WIDTH), BF16),
            pltpu.VMEM((RANK, SLOTS * ROWS), BF16),
            pltpu.VMEM((BINS, RANK, SLOTS * ROWS), BF16),
            pltpu.VMEM((BINS, SLOTS * RANK, SHARD), BF16),
            pltpu.SemaphoreType.DMA((7,)),
            pltpu.SemaphoreType.DMA((2,)),
            pltpu.SemaphoreType.DMA((2,)),
            pltpu.SemaphoreType.DMA((2,)),
            pltpu.SemaphoreType.DMA((2,)),
            pltpu.SemaphoreType.DMA((2,)),
        ],
        compiler_params=pltpu.CompilerParams(
            collective_id=0, has_side_effects=True, vmem_limit_bytes=40 << 20
        ),
        name="owner",
    )(hold(index), hold(documents), counts, hold(up), hold(down), hold(cotangent), hold(qkv))


def sum_kernel(
    index_ref, delta_in, grad_ref, per_up_ref,
    delta_out, down_out, up_out,
    down_sum, up_sum, sem,
):
    delta_copy = pltpu.make_async_copy(delta_in, delta_out, sem.at[0])
    delta_copy.start()
    down_copy = pltpu.make_async_copy(down_sum, down_out, sem.at[1])
    up_copy = pltpu.make_async_copy(up_sum, up_out, sem.at[2])
    up_sum[...] = jnp.zeros_like(up_sum)

    def add_up(owner, _):
        for slot in range(SLOTS):
            up_sum[index_ref[slot, owner]] += per_up_ref[owner * SLOTS + slot]
        return 0

    lax.fori_loop(0, BINS, add_up, 0)
    up_copy.start()
    down_sum[...] = jnp.zeros_like(down_sum)

    def add_down(owner, _):
        for slot in range(SLOTS):
            part = grad_ref[owner, slot * RANK : (slot + 1) * RANK]
            down_sum[index_ref[slot, owner]] += part.astype(F32)
        return 0

    lax.fori_loop(0, BINS, add_down, 0)
    down_copy.start()
    delta_copy.wait()
    up_copy.wait()
    down_copy.wait()


def sum_call(index, delta, grad, per_up):
    vmem, hbm = pl.BlockSpec(memory_space=pltpu.VMEM), pl.BlockSpec(memory_space=pl.ANY)
    adapters = jax.ShapeDtypeStruct((ADAPTERS, RANK, SHARD), F32)
    return pl.pallas_call(
        sum_kernel,
        out_shape=(jax.ShapeDtypeStruct(delta.shape, BF16), adapters, adapters),
        in_specs=[pl.BlockSpec(memory_space=pltpu.SMEM), hbm, vmem, vmem],
        out_specs=(hbm, hbm, hbm),
        scratch_shapes=[
            pltpu.VMEM(adapters.shape, F32),
            pltpu.VMEM(adapters.shape, F32),
            pltpu.SemaphoreType.DMA((3,)),
        ],
        compiler_params=pltpu.CompilerParams(vmem_limit_bytes=16 << 20),
        name="sum",
    )(index, delta, grad, per_up)


def on_device(
    query_key_value_blocks,
    row_document_index,
    counts,
    block_adapter_index,
    lowrank_down_weight,
    lowrank_up_weight,
    cotangent,
):
    index = block_adapter_index[0].T
    up = lowrank_up_weight[0]
    down = lowrank_down_weight[0].transpose(0, 2, 1)
    cot = cotangent.reshape(BLOCKS, ROWS, SHARD)
    grad, delta, per_up = owner_call(
        index, row_document_index[0, 0], counts, up, down, cot, query_key_value_blocks[0, 0]
    )
    delta, grad_down, grad_up = sum_call(index, delta, grad, per_up)
    return (
        delta.reshape(cotangent.shape),
        grad_down.transpose(0, 2, 1)[None],
        grad_up[None],
    )


def solution(mesh):
    in_specs = (
        P("phase", "dp", None, None, None),
        P("phase", "dp", None, None),
        P("phase", "dp"),
        P("phase", None, None),
        P("phase", None, "dp", None),
        P("phase", None, None, "dp"),
        P("phase", None, None, None, "dp"),
    )
    out_specs = (
        P("phase", None, None, None, "dp"),
        P("phase", None, "dp", None),
        P("phase", None, None, "dp"),
    )
    return jax.shard_map(
        on_device, mesh=mesh, in_specs=in_specs, out_specs=out_specs, check_vma=False
    )
```

time: 101 us -> 95.3 us (0.944)
  the two profiles are of different devices: /device:TPU:1 before, /device:TPU:0 now
where the time goes in v2:
time: 95.3 us; the launch traced here: 95.2 us
  Pallas kernels  93.9 us (99%)
  between operations  1.3 us (1%)
    pallas_call x1, Pallas kernels, owner_call(): pl.pallas_call(owner_kernel, out_shape=(jax.ShapeDtypeStruct((BINS, SLOTS...  90 us
    pallas_call x1, Pallas kernels, sum_call(): pl.pallas_call(sum_kernel, out_shape=(jax.ShapeDtypeStruct(delta.shape, B...  3.91 us

profile of v2, /device:TPU:0, one launch (start us, length us, event | category | flops | bytes accessed | tf_op | source)
XLA Modules:
  0.0 95.2 jit_solution(14037893244925474872)
XLA Ops:
  1.3 0.0 copy-start
  1.3 90.0 %owner.1 = (bf16[32,128,256]{2,1,0:T(8,128)(2,1)S(1)}, bf16[64,128,256]{2,1,0:T(8,128)(2,1)S(1)}, f32[64,64,256]{2,1,0:T(8,128)S(1)}) custom-call(s32[2,32]{1,0:T(2,128)} %bitcast.15, s32[2,128]{1,0:T(2,128)} %bitcast.21, s32[1,1]{1,0:T(1,128)S(6)} %copy.10.counts_hbm, bf16[32,64,256]{2,1,0:T(8,128)(2,1)} %bitcast.19, bf16[32,64,256]{2,1,0:T(8,128)(2,1)} %bitcast.20, ...), custom_call_target="tpu_custom_call" | custom-call | tf_op jit(solution)/shard_map/owner/pallas_call | solution.py:233
  91.3 0.0 copy-done
  91.3 3.9 %sum.1 = (bf16[64,128,256]{2,1,0:T(8,128)(2,1)}, f32[32,64,256]{2,1,0:T(8,128)}, f32[32,64,256]{2,1,0:T(8,128)}) custom-call(s32[2,32]{1,0:T(2,128)S(1)} %bitcast.16, bf16[64,128,256]{2,1,0:T(8,128)(2,1)S(1)} %get-tuple-element.9.delta_in, bf16[32,128,256]{2,1,0:T(8,128)(2,1)S(1)} %get-tuple-element.10.grad_ref, f32[64,64,256]{2,1,0:T(8,128)S(1)} %get-tuple-element.11.per_up_ref), custom_call_target="tpu_custom_call" | custom-call | tf_op jit(solution)/shard_map/sum/pallas_call | solution.py:311
Async XLA Ops:
  1.3 90.0 %copy-start = (s32[1,32,2]{1,2,0:T(2,128)S(1)}, s32[1,32,2]{1,2,0:T(2,128)}, u32[]{:S(2)}) copy-start(s32[1,32,2]{1,2,0:T(2,128)} %param.10) | copy-start | bytes 772

commit v3 on v2

--- a/solution.py
+++ b/solution.py
@@ -36,11 +36,20 @@
     )
 
 
-def partner(me, step):
+def displaced(me, step, sign):
+    step = BINS - 1 - step
     kx, turn = step % 4, (step // 4) % 4
     ky, kz = (turn + 4 - kx) % 4, (step // 16 + turn + kx) % 2
     x, y, z = me // 8, (me // 2) % 4, me % 2
-    return ((x + kx) % 4) * 8 + ((y + ky) % 4) * 2 + (z + kz) % 2
+    return ((x + 4 + sign * kx) % 4) * 8 + ((y + 4 + sign * ky) % 4) * 2 + (z + kz) % 2
+
+
+def partner(me, step):
+    return displaced(me, step, 1)
+
+
+def origin(me, step):
+    return displaced(me, step, -1)
 
 
 def owner_kernel(
@@ -48,7 +57,7 @@
     grad_out, delta_out, per_up_out,
     index_ref, counts_ref, up_ref, down_ref, cot, qkv, documents_own, info_own, info_in, bias,
     back_send, back_recv, down_send, down_recv, mixed, scaled, scaled_in, grad_send,
-    load_sem, info_sem, back_sem, down_sem, scaled_sem, grad_sem,
+    load_sem, info_sem, back_sem, down_sem, down_sent, scaled_sem, grad_sem,
 ):
     phase, me = lax.axis_index("phase"), lax.axis_index("dp")
     owners, shards = (phase + SECTIONS - 1) % SECTIONS, (phase + 1) % SECTIONS
@@ -105,9 +114,15 @@
     info_copy = remote(info_own, info_in, info_sem, owners, me)
     info_copy.start()
 
+    def down_copy(to, source):
+        return pltpu.make_async_remote_copy(
+            src_ref=down_send.at[to], dst_ref=down_recv.at[source], send_sem=down_sent, recv_sem=down_sem.at[source],
+            device_id=(owners, to), device_id_type=MESH,
+        )
+
     def send_down(step, _):
         to = partner(me, step)
-        remote(down_send.at[to], down_recv.at[me], down_sem, owners, to).start()
+        down_copy(to, me).start()
         return 0
 
 
@@ -164,25 +179,6 @@
         at = pl.ds(pl.multiple_of(which * SHARD, SHARD), SHARD)
         return mixed[:, :, at].reshape(SLOTS * ROWS, SHARD)
 
-    def project(source, total):
-        return total + dot(down_recv[source], piece(source), 1, 1)
-
-    remote(down_send, down_recv, down_sem, owners, me).wait_recv()
-    projected = lax.fori_loop(
-        0, BINS, project, jnp.zeros((SLOTS * RANK, SLOTS * ROWS), F32), unroll=4
-    )
-    for slot in range(SLOTS):
-        at = slice(slot * ROWS, (slot + 1) * ROWS)
-        own = projected[slot * RANK : (slot + 1) * RANK, at]
-        scaled[:, at] = (LOWRANK_SCALE * own).astype(BF16)
-
-    def send_scaled(step, _):
-        to = partner(me, step)
-        remote(scaled, scaled_in.at[me], scaled_sem, shards, to).start()
-        return 0
-
-    lax.fori_loop(0, BINS, send_scaled, 0)
-
     remote(back_send, back_recv, back_sem, owners, me).wait_recv()
 
     def add_back(source, total):
@@ -199,13 +195,38 @@
         axis=0,
     )
 
+    def make_grad(to, _):
+        grad_send[to] = dot(back_diagonal, piece(to), 1, 0).astype(BF16)
+        return 0
+
+    lax.fori_loop(0, BINS, make_grad, 0, unroll=4)
+
+    def project(step, total):
+        source = origin(me, step)
+        down_copy(source, source).wait_recv()
+        return total + dot(down_recv[source], piece(source), 1, 1)
+
+    projected = lax.fori_loop(
+        0, BINS, project, jnp.zeros((SLOTS * RANK, SLOTS * ROWS), F32), unroll=4
+    )
+    for slot in range(SLOTS):
+        at = slice(slot * ROWS, (slot + 1) * ROWS)
+        own = projected[slot * RANK : (slot + 1) * RANK, at]
+        scaled[:, at] = (LOWRANK_SCALE * own).astype(BF16)
+
+    def send_scaled(step, _):
+        to = partner(me, step)
+        remote(scaled, scaled_in.at[me], scaled_sem, shards, to).start()
+        return 0
+
+    lax.fori_loop(0, BINS, send_scaled, 0)
+
     def send_grad(step, _):
         to = partner(me, step)
-        grad_send[to] = dot(back_diagonal, piece(to), 1, 0).astype(BF16)
         remote(grad_send.at[to], grad_out.at[me], grad_sem, shards, to).start()
         return 0
 
-    lax.fori_loop(0, BINS, send_grad, 0, unroll=4)
+    lax.fori_loop(0, BINS, send_grad, 0)
 
     whole_scaled = remote(back_send, scaled_in, scaled_sem, shards, me)
     whole_scaled.wait_recv()
@@ -221,7 +242,10 @@
     lax.fori_loop(0, BINS, spread, 0, unroll=2)
 
     remote(back_send, back_recv, back_sem, owners, me).wait_send()
-    remote(down_send, down_recv, down_sem, owners, me).wait_send()
+    pltpu.make_async_remote_copy(
+        src_ref=down_send, dst_ref=down_recv, send_sem=down_sent, recv_sem=down_sem.at[0],
+        device_id=(owners, me), device_id_type=MESH,
+    ).wait_send()
     whole_scaled.wait_send()
     whole_grad = remote(grad_send, grad_out, grad_sem, shards, me)
     whole_grad.wait_recv()
@@ -261,7 +285,8 @@
             pltpu.SemaphoreType.DMA((7,)),
             pltpu.SemaphoreType.DMA((2,)),
             pltpu.SemaphoreType.DMA((2,)),
-            pltpu.SemaphoreType.DMA((2,)),
+            pltpu.SemaphoreType.DMA((BINS,)),
+            pltpu.SemaphoreType.DMA,
             pltpu.SemaphoreType.DMA((2,)),
             pltpu.SemaphoreType.DMA((2,)),
         ],
@@ -282,23 +307,18 @@
     down_copy = pltpu.make_async_copy(down_sum, down_out, sem.at[1])
     up_copy = pltpu.make_async_copy(up_sum, up_out, sem.at[2])
     up_sum[...] = jnp.zeros_like(up_sum)
-
-    def add_up(owner, _):
+    down_sum[...] = jnp.zeros_like(down_sum)
+
+    def add(owner, _):
         for slot in range(SLOTS):
-            up_sum[index_ref[slot, owner]] += per_up_ref[owner * SLOTS + slot]
-        return 0
-
-    lax.fori_loop(0, BINS, add_up, 0)
+            adapter = index_ref[slot, owner]
+            up_sum[adapter] += per_up_ref[owner * SLOTS + slot]
+            part = grad_ref[owner, slot * RANK : (slot + 1) * RANK]
+            down_sum[adapter] += part.astype(F32)
+        return 0
+
+    lax.fori_loop(0, BINS, add, 0)
     up_copy.start()
-    down_sum[...] = jnp.zeros_like(down_sum)
-
-    def add_down(owner, _):
-        for slot in range(SLOTS):
-            part = grad_ref[owner, slot * RANK : (slot + 1) * RANK]
-            down_sum[index_ref[slot, owner]] += part.astype(F32)
-        return 0
-
-    lax.fori_loop(0, BINS, add_down, 0)
     down_copy.start()
     delta_copy.wait()
     up_copy.wait()

time: 95.3 us -> 93.5 us (0.981); the launches traced: 95.2 us -> 91.9 us
  Pallas kernels: 93.9 us -> 90.6 us
    pallas_call x1, Pallas kernels: 90 us -> 86.7 us  [owner_call(): pl.pallas_call(owner_kernel, out_shape=(jax.ShapeDtypeStruct((BINS, SLOTS...]
where the time goes in v3:
time: 93.5 us; the launch traced here: 91.9 us
  Pallas kernels  90.6 us (97%)
  between operations  1.3 us (1%)
    pallas_call x1, Pallas kernels, owner_call(): pl.pallas_call(owner_kernel, out_shape=(jax.ShapeDtypeStruct((BINS, SLOTS...  86.7 us
    pallas_call x1, Pallas kernels, sum_call(): pl.pallas_call(sum_kernel, out_shape=(jax.ShapeDtypeStruct(delta.shape, B...  3.91 us

profile of v3, /device:TPU:0, one launch (start us, length us, event | category | flops | bytes accessed | tf_op | source)
XLA Modules:
  0.0 91.9 jit_solution(3231445566951966550)
XLA Ops:
  1.3 0.0 copy-start
  1.3 86.7 %owner.1 = (bf16[32,128,256]{2,1,0:T(8,128)(2,1)S(1)}, bf16[64,128,256]{2,1,0:T(8,128)(2,1)S(1)}, f32[64,64,256]{2,1,0:T(8,128)S(1)}) custom-call(s32[2,32]{1,0:T(2,128)} %bitcast.15, s32[2,128]{1,0:T(2,128)} %bitcast.21, s32[1,1]{1,0:T(1,128)S(6)} %copy.10.counts_hbm, bf16[32,64,256]{2,1,0:T(8,128)(2,1)} %bitcast.19, bf16[32,64,256]{2,1,0:T(8,128)(2,1)} %bitcast.20, ...), custom_call_target="tpu_custom_call" | custom-call | tf_op jit(solution)/shard_map/owner/pallas_call | solution.py:257
  88.0 0.0 copy-done
  88.0 3.9 %sum.1 = (bf16[64,128,256]{2,1,0:T(8,128)(2,1)}, f32[32,64,256]{2,1,0:T(8,128)}, f32[32,64,256]{2,1,0:T(8,128)}) custom-call(s32[2,32]{1,0:T(2,128)S(1)} %bitcast.16, bf16[64,128,256]{2,1,0:T(8,128)(2,1)S(1)} %get-tuple-element.9.delta_in, bf16[32,128,256]{2,1,0:T(8,128)(2,1)S(1)} %get-tuple-element.10.grad_ref, f32[64,64,256]{2,1,0:T(8,128)S(1)} %get-tuple-element.11.per_up_ref), custom_call_target="tpu_custom_call" | custom-call | tf_op jit(solution)/shard_map/sum/pallas_call | solution.py:331
Async XLA Ops:
  1.3 86.7 %copy-start = (s32[1,32,2]{1,2,0:T(2,128)S(1)}, s32[1,32,2]{1,2,0:T(2,128)}, u32[]{:S(2)}) copy-start(s32[1,32,2]{1,2,0:T(2,128)} %param.10) | copy-start | bytes 772

commit v4 on v3

--- a/solution.py
+++ b/solution.py
@@ -101,14 +101,6 @@
     info_own[...] = jnp.full(info_own.shape, counts_ref[0, 0], jnp.int32)
     info_own[:SLOTS] = documents_own[...]
     index_load.wait()
-    down_load.wait()
-
-    def choose_down(to, _):
-        for slot in range(SLOTS):
-            down_send[to, slot * RANK : (slot + 1) * RANK] = down_ref[index_ref[slot, to]]
-        return 0
-
-    lax.fori_loop(0, BINS, choose_down, 0, unroll=4)
 
     pl.semaphore_wait(barrier, BINS)
     info_copy = remote(info_own, info_in, info_sem, owners, me)
@@ -138,6 +130,15 @@
         return 0
 
     lax.fori_loop(0, BINS, send_back, 0, unroll=4)
+
+    down_load.wait()
+
+    def choose_down(to, _):
+        for slot in range(SLOTS):
+            down_send[to, slot * RANK : (slot + 1) * RANK] = down_ref[index_ref[slot, to]]
+        return 0
+
+    lax.fori_loop(0, BINS, choose_down, 0, unroll=4)
 
     lax.fori_loop(0, BINS, send_down, 0)
 

time: 93.5 us -> 93.5 us (level)
  no operation moved by 1% of the time
where the time goes in v4:
time: 93.5 us; the launch traced here: 91.8 us
  Pallas kernels  90.4 us (97%)
  between operations  1.3 us (1%)
    pallas_call x1, Pallas kernels, owner_call(): pl.pallas_call(owner_kernel, out_shape=(jax.ShapeDtypeStruct((BINS, SLOTS...  86.5 us
    pallas_call x1, Pallas kernels, sum_call(): pl.pallas_call(sum_kernel, out_shape=(jax.ShapeDtypeStruct(delta.shape, B...  3.91 us

profile of v4, /device:TPU:0, one launch (start us, length us, event | category | flops | bytes accessed | tf_op | source)
XLA Modules:
  0.0 91.8 jit_solution(4350342125983226609)
XLA Ops:
  1.3 0.0 copy-start
  1.3 86.5 %owner.1 = (bf16[32,128,256]{2,1,0:T(8,128)(2,1)S(1)}, bf16[64,128,256]{2,1,0:T(8,128)(2,1)S(1)}, f32[64,64,256]{2,1,0:T(8,128)S(1)}) custom-call(s32[2,32]{1,0:T(2,128)} %bitcast.15, s32[2,128]{1,0:T(2,128)} %bitcast.21, s32[1,1]{1,0:T(1,128)S(6)} %copy.10.counts_hbm, bf16[32,64,256]{2,1,0:T(8,128)(2,1)} %bitcast.19, bf16[32,64,256]{2,1,0:T(8,128)(2,1)} %bitcast.20, ...), custom_call_target="tpu_custom_call" | custom-call | tf_op jit(solution)/shard_map/owner/pallas_call | solution.py:258
  87.8 0.0 copy-done
  87.8 3.9 %sum.1 = (bf16[64,128,256]{2,1,0:T(8,128)(2,1)}, f32[32,64,256]{2,1,0:T(8,128)}, f32[32,64,256]{2,1,0:T(8,128)}) custom-call(s32[2,32]{1,0:T(2,128)S(1)} %bitcast.16, bf16[64,128,256]{2,1,0:T(8,128)(2,1)S(1)} %get-tuple-element.9.delta_in, bf16[32,128,256]{2,1,0:T(8,128)(2,1)S(1)} %get-tuple-element.10.grad_ref, f32[64,64,256]{2,1,0:T(8,128)S(1)} %get-tuple-element.11.per_up_ref), custom_call_target="tpu_custom_call" | custom-call | tf_op jit(solution)/shard_map/sum/pallas_call | solution.py:332
Async XLA Ops:
  1.3 86.6 %copy-start = (s32[1,32,2]{1,2,0:T(2,128)S(1)}, s32[1,32,2]{1,2,0:T(2,128)}, u32[]{:S(2)}) copy-start(s32[1,32,2]{1,2,0:T(2,128)} %param.10) | copy-start | bytes 772
